TPU v7x, 32 devices: a whole 2x2x4 slice. The times are simulated.
32 devices in a mesh: grp: 4 (over x, core), seq: 8 (over z, y).
Axes of the slice: x: 2, y: 2, z: 4, core: 2. Of those that a mesh axis runs over, the one named last changes fastest.
Arguments:
- queries: bfloat16 [4096, 512], P(('grp', 'seq')), may hold values from -4.5 to 5.5
- key_vectors: bfloat16 [4096, 512], P(('grp', 'seq')), may hold values from -4.5 to 5.5
- value_vectors: bfloat16 [4096, 1024], P(('grp', 'seq')), may hold values from -6 to 6
- input_gate: float32 [4, 4096], P(None, ('grp', 'seq')), may hold values from -4 to 114
- forget_gate: float32 [4, 4096], P(None, ('grp', 'seq')), may hold values from -3 to 25
Outputs:
- hidden_states: bfloat16 [4096, 1024], P(('grp', 'seq'))
All inputs are finite; a program needn't handle non-finite values.
Results may differ from a plain program's by a relative error of at most 0.028.
Values sent between devices are 32-bit elements; how exact they have to be, the bound alone decides.
No kernel may reach another device: no remote copies, remote signals or barrier semaphores. Data moves between devices by JAX's collectives and lax.ppermute only.
A program may use at most 64 MiB of HBM per device.

v0:
```python
import functools

import jax
import jax.numpy as jnp
from jax import lax
from jax.experimental import pallas as pl
from jax.experimental.pallas import tpu as pltpu
from jax.sharding import PartitionSpec as P

floor_value = -1e30
LANES = 128
AXES = ("grp", "seq")


def split_two(x):
    high = x.astype(jnp.bfloat16)
    low = (x - high.astype(jnp.float32)).astype(jnp.bfloat16)
    return high, low


def split_three(x):
    high = x.astype(jnp.bfloat16)
    rest = x - high.astype(jnp.float32)
    mid = rest.astype(jnp.bfloat16)
    low = (rest - mid.astype(jnp.float32)).astype(jnp.bfloat16)
    return high, mid, low


def dot(a, b):
    return jnp.dot(a, b, preferred_element_type=jnp.float32)


def dot_last(a, b):
    return lax.dot_general(a, b, (((1,), (1,)), ((), ())), preferred_element_type=jnp.float32)


def log_forget(forget):
    return jnp.minimum(forget, 0.0) - jnp.log1p(jnp.exp(-jnp.abs(forget)))


def triangle(length, lower):
    rows = lax.broadcasted_iota(jnp.int32, (length, length), 0)
    cols = lax.broadcasted_iota(jnp.int32, (length, length), 1)
    return rows >= cols if lower else rows <= cols


def cumulative_rows(logf):
    ones = triangle(logf.shape[1], False).astype(jnp.bfloat16)
    high, mid, low = split_three(logf)
    return (dot(low, ones) + dot(mid, ones)) + dot(high, ones)


def cumulative_columns(logf):
    ones = triangle(logf.shape[1], True).astype(jnp.bfloat16)
    high, mid, low = split_three(logf)
    return (dot_last(ones, low) + dot_last(ones, mid)) + dot_last(ones, high)


TAIL = 8
VECTOR, TOP, DECAY = range(3)


def member(quad):
    return lax.rem(lax.axis_index(AXES[1]), quad)


def tail_rows(vector, top, decay):
    rest = jnp.zeros((TAIL - 3, vector.shape[1]), jnp.float32)
    return jnp.concatenate([vector, top, decay, rest], axis=0)


def put_state(ref, state, top, decay):
    matrix_rows = ref.shape[0] - TAIL
    ref[0:matrix_rows, :] = state[0:matrix_rows, :]
    place = lax.broadcasted_iota(jnp.int32, (TAIL, ref.shape[1]), 0)
    tail = jnp.where(place == TOP, top, state[matrix_rows:, :])
    ref[matrix_rows:, :] = jnp.where(place == DECAY, decay, tail)


def tail_row(ref, row):
    first = ref.shape[0] - TAIL + row
    return ref[first : first + 1, :]


def state_kernel(k_hbm, v_hbm, in_hbm, fo_hbm, *refs):
    *out_refs, k_ref, v_ref, in_ref, fo_ref, scalar_ref, arrived = refs
    copies = [
        pltpu.make_async_copy(source, target, arrived.at[place])
        for place, (source, target) in enumerate(
            ((fo_hbm, fo_ref), (in_hbm, in_ref), (k_hbm, k_ref), (v_hbm, v_ref))
        )
    ]
    for copy in copies:
        copy.start()
    heads, length = in_ref.shape
    key_dim = k_ref.shape[1] // heads
    value_dim = v_ref.shape[1] // heads
    parts = value_dim // LANES
    copies[0].wait()
    cumul = cumulative_rows(log_forget(fo_ref[...]))
    copies[1].wait()
    level = in_ref[...] - cumul
    level_top = jnp.max(level, axis=1, keepdims=True)
    decay = cumul[:, length - 1 : length]
    scalar_ref[0] = jnp.exp(level - level_top)
    scalar_ref[1] = jnp.broadcast_to(decay + level_top, (heads, length))
    scalar_ref[2] = jnp.broadcast_to(decay, (heads, length))
    copies[2].wait()
    copies[3].wait()
    me = member(heads)
    for step in range(heads):
        head = me ^ step
        keys = k_ref[:, pl.ds(pl.multiple_of(head * key_dim, LANES), key_dim)]
        values = v_ref[:, pl.ds(pl.multiple_of(head * value_dim, LANES), value_dim)]
        row, top, decay = (scalar_ref[place, pl.ds(head, 1), :] for place in range(3))
        high, low = split_two(keys.astype(jnp.float32).T * row)
        matrix = dot(
            jnp.concatenate([high, low], axis=1), jnp.concatenate([values, values], axis=0)
        )
        high, mid, low = split_three(row)
        vector = (dot(low, keys) + dot(mid, keys)) + dot(high, keys)
        for part in range(parts):
            out_ref = out_refs[part * heads + step]
            out_ref[0:key_dim, :] = matrix[:, part * LANES : (part + 1) * LANES]
            out_ref[key_dim:, :] = tail_rows(vector, top, decay)


def read_scalars(refs, scalar_ref, me):
    for step, ref in enumerate(refs):
        scalar_ref[0, pl.ds(me ^ step, 1), :] = tail_row(ref, TOP)
        scalar_ref[1, pl.ds(me ^ step, 1), :] = tail_row(ref, DECAY)
    count = len(refs)
    tops = [scalar_ref[0, place : place + 1, :] for place in range(count)]
    decays = [scalar_ref[1, place : place + 1, :] for place in range(count)]
    return tops, decays


def weights_of(tops, decays):
    moved, total = [], jnp.zeros_like(decays[0])
    for top, decay in zip(reversed(tops), reversed(decays)):
        moved.append(top + total)
        total = total + decay
    moved.reverse()
    joined = functools.reduce(jnp.maximum, moved)
    return [jnp.exp(top - joined) for top in moved], joined, total


def quad_kernel(order, *refs):
    *refs, out_ref, scalar_ref = refs
    refs = [refs[order.index(step)] for step in range(len(order))]
    me = member(len(refs))
    weights, top, decay = weights_of(*read_scalars(refs, scalar_ref, me))
    for place, weight in enumerate(weights):
        scalar_ref[0, place : place + 1, :] = weight
    total = 0.0
    for step, ref in enumerate(refs):
        total = total + scalar_ref[0, pl.ds(me ^ step, 1), :] * ref[...]
    put_state(out_ref, total, top, decay)


def later_side(axis, bit):
    return (lax.axis_index(axis) & bit) != 0


def extend(is_later, other_ref, before_ref):
    other_top = tail_row(other_ref, TOP)
    if before_ref is None:
        decay = jnp.where(is_later, tail_row(other_ref, DECAY), 0.0)
        return (
            jnp.where(is_later, other_ref[...], 0.0),
            jnp.where(is_later, other_top, floor_value),
            decay,
        )
    before_top = tail_row(before_ref, TOP)
    before_decay = tail_row(before_ref, DECAY)
    moved = other_top + before_decay
    top = jnp.where(is_later, jnp.maximum(moved, before_top), before_top)
    other_weight = jnp.where(is_later, jnp.exp(moved - top), 0.0)
    state = other_weight * other_ref[...] + jnp.exp(before_top - top) * before_ref[...]
    decay = jnp.where(is_later, tail_row(other_ref, DECAY), 0.0) + before_decay
    return state, top, decay


def butterfly_kernel(axis, bit, *refs):
    total_ref, other_ref, *before, out_total, out_before = refs
    is_later = later_side(axis, bit)
    own_top, own_decay = tail_row(total_ref, TOP), tail_row(total_ref, DECAY)
    other_top, other_decay = tail_row(other_ref, TOP), tail_row(other_ref, DECAY)
    own_moved = own_top + jnp.where(is_later, 0.0, other_decay)
    other_moved = other_top + jnp.where(is_later, own_decay, 0.0)
    top = jnp.maximum(own_moved, other_moved)
    total = (
        jnp.exp(own_moved - top) * total_ref[...] + jnp.exp(other_moved - top) * other_ref[...]
    )
    put_state(out_total, total, top, own_decay + other_decay)
    put_state(out_before, *extend(is_later, other_ref, before[0] if before else None))


def prefix_kernel(axis, bit, quad, parts, *refs):
    others, befores, refs = refs[:parts], refs[parts : 2 * parts], refs[2 * parts :]
    *refs, scalar_ref, weight_ref = refs
    pieces = [refs[part * quad : (part + 1) * quad] for part in range(parts)]
    out_refs = refs[parts * quad :]
    me = member(quad)
    is_later = later_side(axis, bit)
    starts = [extend(is_later, other, before) for other, before in zip(others, befores)]
    top = starts[0][1]
    tops, decays = read_scalars(pieces[0], scalar_ref, me)
    zero = jnp.zeros_like(top)
    rows = others[0].shape[0]
    for place in range(quad):
        weights, joined, _ = weights_of([top] + tops[:place], [zero] + decays[:place])
        weights += [zero] * (quad - place)
        for index, weight in enumerate(weights):
            weight_ref[place, index : index + 1, :] = weight
        scalar_ref[0, place : place + 1, :] = joined
    for step, out_ref in enumerate(out_refs):
        place = me ^ step
        weights = [weight_ref[place, pl.ds(1 + (me ^ index), 1), :] for index in range(quad)]
        for part, (start, _, _) in enumerate(starts):
            state = weight_ref[place, 0:1, :] * start
            for weight, piece in zip(weights, pieces[part]):
                state = state + weight * piece[...]
            first = part * (rows - TAIL)
            out_ref[first : first + rows - TAIL, :] = state[0 : rows - TAIL, :]
        vector = state[rows - TAIL : rows - TAIL + 1, :]
        tail = tail_rows(vector, scalar_ref[0, pl.ds(place, 1), :], zero)
        out_ref[out_ref.shape[0] - TAIL :, :] = tail


CUMUL, ROW_LEVEL, INNER_DEN = range(3)


def inner_kernel(q_ref, k_ref, v_ref, in_ref, fo_ref, num_ref, stat_ref):
    heads, length = in_ref.shape
    key_dim = q_ref.shape[1] // heads
    value_dim = v_ref.shape[1] // heads
    logf = log_forget(fo_ref[...])
    level = in_ref[...] - cumulative_rows(logf)
    cumul = cumulative_columns(logf)
    causal = triangle(length, True)
    for head in range(heads):
        queries = q_ref[:, head * key_dim : (head + 1) * key_dim]
        keys = k_ref[:, head * key_dim : (head + 1) * key_dim]
        values = v_ref[:, head * value_dim : (head + 1) * value_dim]
        scores = dot_last(queries, keys) * (key_dim**-0.5)
        masked = jnp.where(causal, level[head : head + 1, :], -jnp.inf)
        row_level = jnp.max(masked, axis=1, keepdims=True)
        weighted = jnp.exp(masked - row_level) * scores
        stat_ref[head, :, CUMUL : CUMUL + 1] = cumul[:, head : head + 1]
        stat_ref[head, :, ROW_LEVEL : ROW_LEVEL + 1] = row_level
        stat_ref[head, :, INNER_DEN : INNER_DEN + 1] = jnp.sum(weighted, axis=1, keepdims=True)
        num_ref[head] = dot(weighted.astype(jnp.bfloat16), values)


def add_carried(head, q_ref, num_ref, stat_ref, message_ref):
    length, value_dim = num_ref.shape[1:]
    key_dim = q_ref.shape[1] // num_ref.shape[0]
    parts = value_dim // LANES
    scaling = key_dim**-0.5
    query = q_ref[:, pl.ds(pl.multiple_of(head * key_dim, LANES), key_dim)]
    matrix = jnp.concatenate(
        [message_ref[part * key_dim : (part + 1) * key_dim, :] for part in range(parts)], 1
    )
    high, low = split_two(matrix)
    carried = dot(jnp.concatenate([query, query], axis=1), jnp.concatenate([high, low], axis=0))
    stats = stat_ref[head]
    cumul, row_level, inner_den = (stats[:, place : place + 1] for place in range(3))
    top = tail_row(message_ref, TOP)[:, 0:1]
    carried_den = jnp.sum(
        query.astype(jnp.float32) * tail_row(message_ref, VECTOR), axis=1, keepdims=True
    )
    joined = jnp.maximum(row_level, top)
    inner_factor = jnp.exp(row_level - joined)
    outer_factor = jnp.exp(top - joined) * scaling
    denom = inner_factor * inner_den + outer_factor * carried_den
    inverse = 1.0 / jnp.maximum(jnp.abs(denom), jnp.exp(-(cumul + joined)))
    return (inner_factor * inverse) * num_ref[head] + (outer_factor * inverse) * carried


def part_kernel(steps, q_ref, num_ref, stat_ref, *refs):
    me = member(num_ref.shape[0])
    count = len(steps)
    for step, message_ref, out_ref in zip(steps, refs[:count], refs[count:]):
        head = me ^ step
        out_ref[...] = add_carried(head, q_ref, num_ref, stat_ref, message_ref).astype(
            out_ref.dtype
        )


def last_kernel(q_ref, num_ref, stat_ref, message_ref, *refs):
    *done_refs, out_hbm, own_ref, done = refs
    heads, _, value_dim = num_ref.shape
    me = member(heads)

    def place(step, source):
        columns = pl.ds(pl.multiple_of((me ^ step) * value_dim, LANES), value_dim)
        copy = pltpu.make_async_copy(source, out_hbm.at[:, columns], done.at[step])
        copy.start()
        return copy

    copies = [place(step, ref) for step, ref in enumerate(done_refs)]
    own_ref[...] = add_carried(me ^ (heads - 1), q_ref, num_ref, stat_ref, message_ref).astype(
        own_ref.dtype
    )
    copies.append(place(heads - 1, own_ref))
    for copy in copies:
        copy.wait()


def swap(array, axis, step):
    count = lax.axis_size(axis)
    return lax.ppermute(array, axis, [(place, place ^ step) for place in range(count)])


def exchange(pieces):
    return [pieces[0]] + [
        swap(pieces[step], AXES[1], step) for step in range(1, len(pieces))
    ]


def on_device(groups, group_length, queries, key_vectors, value_vectors, input_gate, forget_gate):
    heads, length = input_gate.shape
    key_dim = queries.shape[1] // heads
    value_dim = value_vectors.shape[1] // heads
    parts = value_dim // LANES
    whole = jax.ShapeDtypeStruct((parts * key_dim + TAIL, LANES), jnp.float32)
    message = jax.ShapeDtypeStruct((key_dim + TAIL, LANES), jnp.float32)
    messages = (message,) * heads
    params = pltpu.CompilerParams(vmem_limit_bytes=48 * 1024 * 1024)
    hbm = pl.BlockSpec(memory_space=pltpu.HBM)
    scalars = pltpu.VMEM((3, heads, LANES), jnp.float32)
    output = jax.ShapeDtypeStruct((length, heads * value_dim), jnp.bfloat16)
    operands = (key_vectors, value_vectors, input_gate, forget_gate)
    levels = []
    for axis, bit, size in ((AXES[1], heads, group_length), (AXES[0], 1, groups)):
        while bit < size:
            levels.append((axis, bit))
            bit *= 2

    own = pl.pallas_call(
        state_kernel,
        out_shape=messages * parts,
        in_specs=[hbm] * len(operands),
        scratch_shapes=[pltpu.VMEM(array.shape, array.dtype) for array in operands]
        + [scalars, pltpu.SemaphoreType.DMA((len(operands),))],
        compiler_params=params,
    )(*(pltpu.with_memory_space_constraint(array, pltpu.HBM) for array in operands))
    inner_num, stats = pl.pallas_call(
        inner_kernel,
        out_shape=(
            jax.ShapeDtypeStruct((heads, length, value_dim), jnp.float32),
            jax.ShapeDtypeStruct((heads, length, 3), jnp.float32),
        ),
        compiler_params=params,
    )(queries, *operands)
    pieces = [exchange(own[part * heads : (part + 1) * heads]) for part in range(parts)]
    totals = []
    for part, chunk in enumerate(pieces):
        order = list(range(heads)) if part else [0, heads - 1, *range(1, heads - 1)]
        totals.append(
            pl.pallas_call(
                functools.partial(quad_kernel, order),
                out_shape=message,
                scratch_shapes=[scalars],
                compiler_params=params,
            )(*(chunk[step] for step in order))
        )
    before = [[] for _ in range(parts)]
    for axis, bit in levels[:-1]:
        join_level = pl.pallas_call(
            functools.partial(butterfly_kernel, axis, bit),
            out_shape=(message, message),
            compiler_params=params,
        )
        others = [swap(array, axis, bit) for array in totals]
        for part in range(parts):
            totals[part], *before[part] = join_level(totals[part], others[part], *before[part])
    others = [swap(array, *levels[-1]) for array in totals]
    starts = []
    for part in range(parts):
        starts += before[part]
    states = pl.pallas_call(
        functools.partial(prefix_kernel, *levels[-1], heads, parts),
        out_shape=(whole,) * heads,
        scratch_shapes=[scalars, pltpu.VMEM((heads, 1 + heads, LANES), jnp.float32)],
        compiler_params=params,
    )(*others, *starts, *(piece for chunk in pieces for piece in chunk))
    carried = exchange(states)
    column = jax.ShapeDtypeStruct((length, value_dim), output.dtype)
    columns = []
    for steps in [(0, 1)] + [(step,) for step in range(2, heads - 1)]:
        columns += pl.pallas_call(
            functools.partial(part_kernel, steps),
            out_shape=(column,) * len(steps),
            compiler_params=params,
        )(queries, inner_num, stats, *(carried[step] for step in steps))
    return pl.pallas_call(
        last_kernel,
        out_shape=output,
        out_specs=hbm,
        scratch_shapes=[
            pltpu.VMEM(column.shape, column.dtype),
            pltpu.SemaphoreType.DMA((heads,)),
        ],
        compiler_params=params,
    )(queries, inner_num, stats, carried[-1], *columns)


def solution(mesh):
    return jax.shard_map(
        functools.partial(on_device, mesh.shape["grp"], mesh.shape["seq"]),
        mesh=mesh,
        in_specs=(
            P(AXES, None),
            P(AXES, None),
            P(AXES, None),
            P(None, AXES),
            P(None, AXES),
        ),
        out_specs=P(AXES, None),
        check_vma=False,
    )
```

profile of v0, /device:TPU:0, one launch (start us, length us, event | category | flops | bytes accessed | tf_op | source)
XLA Modules:
  0.0 36.7 jit_solution(9477742998284546452)
XLA Ops:
  0.0 1.4 %shard_map.56 = (f32[136,128]{1,0:T(8,128)S(1)}, f32[136,128]{1,0:T(8,128)S(1)}, f32[136,128]{1,0:T(8,128)S(1)}, f32[136,128]{1,0:T(8,128)S(1)}, f32[136,128]{1,...) custom-call(bf16[128,512]{1,0:T(8,128)(2,1)} %k_hbm.1, ...), custom_call_target="tpu_custom_call" | custom-call | tf_op jit(solution)/shard_map/pallas_call | solution.py:341
  1.5 3.0 %collective-permute-start.6 = (f32[136,128]{1,0:T(8,128)S(1)}, f32[136,128]{1,0:T(8,128)S(1)}, u32[]{:S(2)}, u32[]{:S(2)}) collective-permute-start(f32[136,128]{1,0:T(8,128)S(1)} %get-tuple-element.39), channel_id=1, source_target_pairs={{0,1},{1,0},{2,3},{3,2},{4,5},{5,4},{6,7},{7,6},{8,9},{9,8},{10,11... | collective-permute-start | bytes 208904 | tf_op jit(solution)/shard_map/ppermute | solution.py:313
  4.5 1.6 %collective-permute-start.7 = (f32[136,128]{1,0:T(8,128)S(1)}, f32[136,128]{1,0:T(8,128)S(1)}, u32[]{:S(2)}, u32[]{:S(2)}) collective-permute-start(f32[136,128]{1,0:T(8,128)S(1)} %get-tuple-element.40), channel_id=1, source_target_pairs={{0,2},{1,3},{2,0},{3,1},{4,6},{5,7},{6,4},{7,5},{8,10},{9,11},{10,... | collective-permute-start | bytes 208904 | tf_op jit(solution)/shard_map/ppermute | solution.py:313
  6.1 0.0 collective-permute-start.8
  6.1 2.9 %collective-permute-start = (f32[136,128]{1,0:T(8,128)S(1)}, f32[136,128]{1,0:T(8,128)S(1)}, u32[]{:S(2)}, u32[]{:S(2)}) collective-permute-start(f32[136,128]{1,0:T(8,128)S(1)} %get-tuple-element.32), channel_id=1, source_target_pairs={{0,3},{1,2},{2,1},{3,0},{4,7},{5,6},{6,5},{7,4},{8,11},{9,10},{10,... | collective-permute-start | bytes 208904 | tf_op jit(solution)/shard_map/ppermute | solution.py:313
  9.0 0.5 %collective-permute-start.1 = (f32[136,128]{1,0:T(8,128)S(1)}, f32[136,128]{1,0:T(8,128)S(1)}, u32[]{:S(2)}, u32[]{:S(2)}) collective-permute-start(f32[136,128]{1,0:T(8,128)S(1)} %get-tuple-element.33), channel_id=1, source_target_pairs={{0,1},{1,0},{2,3},{3,2},{4,5},{5,4},{6,7},{7,6},{8,9},{9,8},{10,11... | collective-permute-start | bytes 208904 | tf_op jit(solution)/shard_map/ppermute | solution.py:313
  9.5 0.0 collective-permute-done.6.refs_1_.refs_9_
  9.5 0.1 collective-permute-start.2
  9.6 0.0 collective-permute-done.7.refs_2_.refs_10_
  9.6 1.7 %collective-permute-done.8.refs_3_.refs_11_ = f32[136,128]{1,0:T(8,128)S(1)} collective-permute-done((f32[136,128]{1,0:T(8,128)S(1)}, f32[136,128]{1,0:T(8,128)S(1)}, u32[]{:S(2)}, u32[]{:S(2)}) %collective-permute-start.8) | collective-permute-done | bytes 69664 | tf_op jit(solution)/shard_map/ppermute | solution.py:313
  11.3 0.1 shard_map.60.refs_0_
  11.4 2.7 %collective-permute-start.9 = (f32[136,128]{1,0:T(8,128)S(1)}, f32[136,128]{1,0:T(8,128)S(1)}, u32[]{:S(2)}, u32[]{:S(2)}) collective-permute-start(f32[136,128]{1,0:T(8,128)S(1)} %shard_map.60.refs_0_), channel_id=1, source_target_pairs={{0,4},{1,5},{2,6},{3,7},{4,0},{5,1},{6,2},{7,3},{8,12},{9,13},{10,... | collective-permute-start | bytes 208904 | tf_op jit(solution)/shard_map/ppermute | solution.py:313
  14.0 0.0 collective-permute-done.refs_1_.refs_7_
  14.0 0.0 collective-permute-done.1.refs_2_.refs_5_
  14.0 0.5 %collective-permute-done.2.refs_3_.refs_6_ = f32[136,128]{1,0:T(8,128)S(1)} collective-permute-done((f32[136,128]{1,0:T(8,128)S(1)}, f32[136,128]{1,0:T(8,128)S(1)}, u32[]{:S(2)}, u32[]{:S(2)}) %collective-permute-start.2) | collective-permute-done | bytes 69664 | tf_op jit(solution)/shard_map/ppermute | solution.py:313
  14.5 0.1 shard_map.57.refs_0_
  14.6 2.0 %collective-permute-start.3 = (f32[136,128]{1,0:T(8,128)S(1)}, f32[136,128]{1,0:T(8,128)S(1)}, u32[]{:S(2)}, u32[]{:S(2)}) collective-permute-start(f32[136,128]{1,0:T(8,128)S(1)} %shard_map.57.refs_0_), channel_id=1, source_target_pairs={{0,4},{1,5},{2,6},{3,7},{4,0},{5,1},{6,2},{7,3},{8,12},{9,13},{10,... | collective-permute-start | bytes 208904 | tf_op jit(solution)/shard_map/ppermute | solution.py:313
  16.6 2.0 %collective-permute-done.9.refs_1_ = f32[136,128]{1,0:T(8,128)S(1)} collective-permute-done((f32[136,128]{1,0:T(8,128)S(1)}, f32[136,128]{1,0:T(8,128)S(1)}, u32[]{:S(2)}, u32[]{:S(2)}) %collective-permute-start.9) | collective-permute-done | bytes 69664 | tf_op jit(solution)/shard_map/ppermute | solution.py:313
  18.6 0.1 collective-permute-start.10
  18.7 1.9 %collective-permute-done.3.refs_1_ = f32[136,128]{1,0:T(8,128)S(1)} collective-permute-done((f32[136,128]{1,0:T(8,128)S(1)}, f32[136,128]{1,0:T(8,128)S(1)}, u32[]{:S(2)}, u32[]{:S(2)}) %collective-permute-start.3) | collective-permute-done | bytes 69664 | tf_op jit(solution)/shard_map/ppermute | solution.py:313
  20.6 0.1 collective-permute-start.4
  20.7 0.0 collective-permute-done.10.refs_1_
  20.8 1.6 %collective-permute-start.11 = (f32[136,128]{1,0:T(8,128)S(1)}, f32[136,128]{1,0:T(8,128)S(1)}, u32[]{:S(2)}, u32[]{:S(2)}) collective-permute-start(f32[136,128]{1,0:T(8,128)S(1)} %get-tuple-element.44), channel_id=1, source_target_pairs={{0,16},{8,24},{16,0},{24,8},{1,17},{9,25},{17,1},{25,9},{2,18},{10... | collective-permute-start | bytes 208904 | tf_op jit(solution)/shard_map/ppermute | solution.py:313
  22.3 0.0 collective-permute-done.4.refs_1_
  22.4 1.2 %collective-permute-start.5 = (f32[136,128]{1,0:T(8,128)S(1)}, f32[136,128]{1,0:T(8,128)S(1)}, u32[]{:S(2)}, u32[]{:S(2)}) collective-permute-start(f32[136,128]{1,0:T(8,128)S(1)} %get-tuple-element.37), channel_id=1, source_target_pairs={{0,16},{8,24},{16,0},{24,8},{1,17},{9,25},{17,1},{25,9},{2,18},{10... | collective-permute-start | bytes 208904 | tf_op jit(solution)/shard_map/ppermute | solution.py:313
  23.5 2.0 %collective-permute-done.11.refs_1_ = f32[136,128]{1,0:T(8,128)S(1)} collective-permute-done((f32[136,128]{1,0:T(8,128)S(1)}, f32[136,128]{1,0:T(8,128)S(1)}, u32[]{:S(2)}, u32[]{:S(2)}) %collective-permute-start.11) | collective-permute-done | bytes 69664 | tf_op jit(solution)/shard_map/ppermute | solution.py:313
  25.6 1.3 %collective-permute-done.5.refs_0_ = f32[136,128]{1,0:T(8,128)S(1)} collective-permute-done((f32[136,128]{1,0:T(8,128)S(1)}, f32[136,128]{1,0:T(8,128)S(1)}, u32[]{:S(2)}, u32[]{:S(2)}) %collective-permute-start.5) | collective-permute-done | bytes 69664 | tf_op jit(solution)/shard_map/ppermute | solution.py:313
  26.9 0.0 copy-start
  26.9 0.0 copy-start.1
  26.9 0.0 copy-start.2
  26.9 0.2 shard_map.63
  27.1 0.0 copy-start.4
  27.1 0.0 copy-start.3
  27.2 0.2 collective-permute-start.14
  27.4 1.0 %collective-permute-start.13 = (f32[264,128]{1,0:T(8,128)S(1)}, f32[264,128]{1,0:T(8,128)S(1)}, u32[]{:S(2)}, u32[]{:S(2)}) collective-permute-start(f32[264,128]{1,0:T(8,128)S(1)} %get-tuple-element.49), channel_id=1, source_target_pairs={{0,1},{1,0},{2,3},{3,2},{4,5},{5,4},{6,7},{7,6},{8,9},{9,8},{10,11... | collective-permute-start | bytes 405512 | tf_op jit(solution)/shard_map/ppermute | solution.py:313
  28.3 2.4 %collective-permute-start.12 = (f32[264,128]{1,0:T(8,128)S(1)}, f32[264,128]{1,0:T(8,128)S(1)}, u32[]{:S(2)}, u32[]{:S(2)}) collective-permute-start(f32[264,128]{1,0:T(8,128)S(1)} %get-tuple-element.47), channel_id=1, source_target_pairs={{0,3},{1,2},{2,1},{3,0},{4,7},{5,6},{6,5},{7,4},{8,11},{9,10},{10,... | collective-permute-start | bytes 405512 | tf_op jit(solution)/shard_map/ppermute | solution.py:313
  30.7 0.0 copy-done
  30.7 0.0 copy-done.1
  30.7 0.0 copy-done.2
  30.7 0.0 copy-done.4
  30.7 0.0 copy-done.3
  30.7 0.9 %shard_map.55 = (f32[4,128,256]{2,1,0:T(8,128)S(1)}, f32[4,128,3]{2,1,0:T(8,128)S(1)}) custom-call(bf16[128,512]{1,0:T(8,128)(2,1)S(1)} %copy-done, bf16[128,512]{1,0:T(8,128)(2,1)S(1)} %copy-done.2, bf16[128,1024]{1,0:T(8,128)(2,1)S(1)} %copy-done.1, f32[4,128]{1,0:T(4,128)S(1)} %copy-done.3, f32[4,128]{1,0:T(4,128)S(1)} %copy-done.4), custom_call_target="tpu_custom_call" | custom-call | tf_op jit(solution)/shard_map/pallas_call | solution.py:349
  31.6 2.1 %collective-permute-done.14.refs_0_ = f32[264,128]{1,0:T(8,128)S(1)} collective-permute-done((f32[264,128]{1,0:T(8,128)S(1)}, f32[264,128]{1,0:T(8,128)S(1)}, u32[]{:S(2)}, u32[]{:S(2)}) %collective-permute-start.14) | collective-permute-done | bytes 135200 | tf_op jit(solution)/shard_map/ppermute | solution.py:313
  33.7 0.4 %shard_map.65.refs_2_ = bf16[128,256]{1,0:T(8,128)(2,1)S(1)} custom-call(bf16[128,512]{1,0:T(8,128)(2,1)S(1)} %copy-done, f32[4,128,256]{2,1,0:T(8,128)S(1)} %get-tuple-element.29.num_ref, f32[4,128,3]{2,1,0:T(8,128)S(1)} %get-tuple-element.30.stat_ref, f32[264,128]{1,0:T(8,128)S(1)} %collective-permute-done.14.refs_0_), custom_call_target="tpu_custom_call" | custom-call | tf_op jit(solution)/shard_map/pallas_call | solution.py:393
  34.1 0.0 collective-permute-done.13.refs_1_
  34.1 0.6 %shard_map.64 = (bf16[128,256]{1,0:T(8,128)(2,1)S(1)}, bf16[128,256]{1,0:T(8,128)(2,1)S(1)}) custom-call(bf16[128,512]{1,0:T(8,128)(2,1)S(1)} %copy-done, f32[4,128,256]{2,1,0:T(8,128)S(1)} %get-tuple-element.29.num_ref, f32[4,128,3]{2,1,0:T(8,128)S(1)} %get-tuple-element.30.stat_ref, f32[264,128]{1,0:T(8,128)S(1)} %get-tuple-element.48.refs_0_, ...), custom_call_target="tpu_custom_call" | custom-call | tf_op jit(solution)/shard_map/pallas_call | solution.py:393
  34.7 0.9 %collective-permute-done.12.message_ref = f32[264,128]{1,0:T(8,128)S(1)} collective-permute-done((f32[264,128]{1,0:T(8,128)S(1)}, f32[264,128]{1,0:T(8,128)S(1)}, u32[]{:S(2)}, u32[]{:S(2)}) %collective-permute-start.12) | collective-permute-done | bytes 135200 | tf_op jit(solution)/shard_map/ppermute | solution.py:313
  35.6 1.1 %shard_map.66 = bf16[128,1024]{1,0:T(8,128)(2,1)} custom-call(bf16[128,512]{1,0:T(8,128)(2,1)S(1)} %copy-done, f32[4,128,256]{2,1,0:T(8,128)S(1)} %get-tuple-element.29.num_ref, f32[4,128,3]{2,1,0:T(8,128)S(1)} %get-tuple-element.30.stat_ref, f32[264,128]{1,0:T(8,128)S(1)} %collective-permute-done.12.message_ref, ...), custom_call_target="tpu_custom_call" | custom-call | tf_op jit(solution)/shard_map/pallas_call | solution.py:398
  (4 shorter events, 0.1 us)
Async XLA Ops:
  1.5 8.0 %collective-permute-start.6 = (f32[136,128]{1,0:T(8,128)S(1)}, f32[136,128]{1,0:T(8,128)S(1)}, u32[]{:S(2)}, u32[]{:S(2)}) collective-permute-start(f32[136,128]{1,0:T(8,128)S(1)} %get-tuple-element.39), channel_id=1, source_target_pairs={{0,1},{1,0},{2,3},{3,2},{4,5},{5,4},{6,7},{7,6},{8,9},{9,8},{10,11... | collective-permute-start | bytes 208904 | tf_op jit(solution)/shard_map/ppermute | solution.py:313
  4.5 5.1 %collective-permute-start.7 = (f32[136,128]{1,0:T(8,128)S(1)}, f32[136,128]{1,0:T(8,128)S(1)}, u32[]{:S(2)}, u32[]{:S(2)}) collective-permute-start(f32[136,128]{1,0:T(8,128)S(1)} %get-tuple-element.40), channel_id=1, source_target_pairs={{0,2},{1,3},{2,0},{3,1},{4,6},{5,7},{6,4},{7,5},{8,10},{9,11},{10,... | collective-permute-start | bytes 208904 | tf_op jit(solution)/shard_map/ppermute | solution.py:313
  6.1 5.3 %collective-permute-start.8 = (f32[136,128]{1,0:T(8,128)S(1)}, f32[136,128]{1,0:T(8,128)S(1)}, u32[]{:S(2)}, u32[]{:S(2)}) collective-permute-start(f32[136,128]{1,0:T(8,128)S(1)} %get-tuple-element.41), channel_id=1, source_target_pairs={{0,3},{1,2},{2,1},{3,0},{4,7},{5,6},{6,5},{7,4},{8,11},{9,10},{10,... | collective-permute-start | bytes 208904 | tf_op jit(solution)/shard_map/ppermute | solution.py:313
  6.1 8.0 %collective-permute-start = (f32[136,128]{1,0:T(8,128)S(1)}, f32[136,128]{1,0:T(8,128)S(1)}, u32[]{:S(2)}, u32[]{:S(2)}) collective-permute-start(f32[136,128]{1,0:T(8,128)S(1)} %get-tuple-element.32), channel_id=1, source_target_pairs={{0,3},{1,2},{2,1},{3,0},{4,7},{5,6},{6,5},{7,4},{8,11},{9,10},{10,... | collective-permute-start | bytes 208904 | tf_op jit(solution)/shard_map/ppermute | solution.py:313
  9.0 5.1 %collective-permute-start.1 = (f32[136,128]{1,0:T(8,128)S(1)}, f32[136,128]{1,0:T(8,128)S(1)}, u32[]{:S(2)}, u32[]{:S(2)}) collective-permute-start(f32[136,128]{1,0:T(8,128)S(1)} %get-tuple-element.33), channel_id=1, source_target_pairs={{0,1},{1,0},{2,3},{3,2},{4,5},{5,4},{6,7},{7,6},{8,9},{9,8},{10,11... | collective-permute-start | bytes 208904 | tf_op jit(solution)/shard_map/ppermute | solution.py:313
  9.5 5.0 %collective-permute-start.2 = (f32[136,128]{1,0:T(8,128)S(1)}, f32[136,128]{1,0:T(8,128)S(1)}, u32[]{:S(2)}, u32[]{:S(2)}) collective-permute-start(f32[136,128]{1,0:T(8,128)S(1)} %get-tuple-element.34), channel_id=1, source_target_pairs={{0,2},{1,3},{2,0},{3,1},{4,6},{5,7},{6,4},{7,5},{8,10},{9,11},{10,... | collective-permute-start | bytes 208904 | tf_op jit(solution)/shard_map/ppermute | solution.py:313
  11.4 7.2 %collective-permute-start.9 = (f32[136,128]{1,0:T(8,128)S(1)}, f32[136,128]{1,0:T(8,128)S(1)}, u32[]{:S(2)}, u32[]{:S(2)}) collective-permute-start(f32[136,128]{1,0:T(8,128)S(1)} %shard_map.60.refs_0_), channel_id=1, source_target_pairs={{0,4},{1,5},{2,6},{3,7},{4,0},{5,1},{6,2},{7,3},{8,12},{9,13},{10,... | collective-permute-start | bytes 208904 | tf_op jit(solution)/shard_map/ppermute | solution.py:313
  14.6 6.0 %collective-permute-start.3 = (f32[136,128]{1,0:T(8,128)S(1)}, f32[136,128]{1,0:T(8,128)S(1)}, u32[]{:S(2)}, u32[]{:S(2)}) collective-permute-start(f32[136,128]{1,0:T(8,128)S(1)} %shard_map.57.refs_0_), channel_id=1, source_target_pairs={{0,4},{1,5},{2,6},{3,7},{4,0},{5,1},{6,2},{7,3},{8,12},{9,13},{10,... | collective-permute-start | bytes 208904 | tf_op jit(solution)/shard_map/ppermute | solution.py:313
  18.6 2.1 %collective-permute-start.10 = (f32[136,128]{1,0:T(8,128)S(1)}, f32[136,128]{1,0:T(8,128)S(1)}, u32[]{:S(2)}, u32[]{:S(2)}) collective-permute-start(f32[136,128]{1,0:T(8,128)S(1)} %get-tuple-element.42.refs_0_), channel_id=1, source_target_pairs={{0,8},{8,0},{16,24},{24,16},{1,9},{9,1},{17,25},{25,17},{2,10},{10... | collective-permute-start | bytes 208904 | tf_op jit(solution)/shard_map/ppermute | solution.py:313
  20.6 1.7 %collective-permute-start.4 = (f32[136,128]{1,0:T(8,128)S(1)}, f32[136,128]{1,0:T(8,128)S(1)}, u32[]{:S(2)}, u32[]{:S(2)}) collective-permute-start(f32[136,128]{1,0:T(8,128)S(1)} %get-tuple-element.35.refs_0_), channel_id=1, source_target_pairs={{0,8},{8,0},{16,24},{24,16},{1,9},{9,1},{17,25},{25,17},{2,10},{10... | collective-permute-start | bytes 208904 | tf_op jit(solution)/shard_map/ppermute | solution.py:313
  20.8 4.8 %collective-permute-start.11 = (f32[136,128]{1,0:T(8,128)S(1)}, f32[136,128]{1,0:T(8,128)S(1)}, u32[]{:S(2)}, u32[]{:S(2)}) collective-permute-start(f32[136,128]{1,0:T(8,128)S(1)} %get-tuple-element.44), channel_id=1, source_target_pairs={{0,16},{8,24},{16,0},{24,8},{1,17},{9,25},{17,1},{25,9},{2,18},{10... | collective-permute-start | bytes 208904 | tf_op jit(solution)/shard_map/ppermute | solution.py:313
  22.4 4.5 %collective-permute-start.5 = (f32[136,128]{1,0:T(8,128)S(1)}, f32[136,128]{1,0:T(8,128)S(1)}, u32[]{:S(2)}, u32[]{:S(2)}) collective-permute-start(f32[136,128]{1,0:T(8,128)S(1)} %get-tuple-element.37), channel_id=1, source_target_pairs={{0,16},{8,24},{16,0},{24,8},{1,17},{9,25},{17,1},{25,9},{2,18},{10... | collective-permute-start | bytes 208904 | tf_op jit(solution)/shard_map/ppermute | solution.py:313
  26.9 3.8 %copy-start = (bf16[128,512]{1,0:T(8,128)(2,1)S(1)}, bf16[128,512]{1,0:T(8,128)(2,1)}, u32[]{:S(2)}) copy-start(bf16[128,512]{1,0:T(8,128)(2,1)} %q_ref.7) | copy-start | bytes 393220
  26.9 3.8 %copy-start.1 = (bf16[128,1024]{1,0:T(8,128)(2,1)S(1)}, bf16[128,1024]{1,0:T(8,128)(2,1)}, u32[]{:S(2)}) copy-start(bf16[128,1024]{1,0:T(8,128)(2,1)} %v_hbm.1) | copy-start | bytes 786436
  26.9 3.8 %copy-start.2 = (bf16[128,512]{1,0:T(8,128)(2,1)S(1)}, bf16[128,512]{1,0:T(8,128)(2,1)}, u32[]{:S(2)}) copy-start(bf16[128,512]{1,0:T(8,128)(2,1)} %k_hbm.1) | copy-start | bytes 393220
  27.1 3.6 %copy-start.4 = (f32[4,128]{1,0:T(4,128)S(1)}, f32[4,128]{1,0:T(4,128)}, u32[]{:S(2)}) copy-start(f32[4,128]{1,0:T(4,128)} %fo_hbm.1) | copy-start | bytes 6148
  27.1 3.6 %copy-start.3 = (f32[4,128]{1,0:T(4,128)S(1)}, f32[4,128]{1,0:T(4,128)}, u32[]{:S(2)}) copy-start(f32[4,128]{1,0:T(4,128)} %in_hbm.1) | copy-start | bytes 6148
  27.2 6.6 %collective-permute-start.14 = (f32[264,128]{1,0:T(8,128)S(1)}, f32[264,128]{1,0:T(8,128)S(1)}, u32[]{:S(2)}, u32[]{:S(2)}) collective-permute-start(f32[264,128]{1,0:T(8,128)S(1)} %get-tuple-element.52), channel_id=1, source_target_pairs={{0,2},{1,3},{2,0},{3,1},{4,6},{5,7},{6,4},{7,5},{8,10},{9,11},{10,... | collective-permute-start | bytes 405512 | tf_op jit(solution)/shard_map/ppermute | solution.py:313
  27.4 6.7 %collective-permute-start.13 = (f32[264,128]{1,0:T(8,128)S(1)}, f32[264,128]{1,0:T(8,128)S(1)}, u32[]{:S(2)}, u32[]{:S(2)}) collective-permute-start(f32[264,128]{1,0:T(8,128)S(1)} %get-tuple-element.49), channel_id=1, source_target_pairs={{0,1},{1,0},{2,3},{3,2},{4,5},{5,4},{6,7},{7,6},{8,9},{9,8},{10,11... | collective-permute-start | bytes 405512 | tf_op jit(solution)/shard_map/ppermute | solution.py:313
  28.3 7.3 %collective-permute-start.12 = (f32[264,128]{1,0:T(8,128)S(1)}, f32[264,128]{1,0:T(8,128)S(1)}, u32[]{:S(2)}, u32[]{:S(2)}) collective-permute-start(f32[264,128]{1,0:T(8,128)S(1)} %get-tuple-element.47), channel_id=1, source_target_pairs={{0,3},{1,2},{2,1},{3,0},{4,7},{5,6},{6,5},{7,4},{8,11},{9,10},{10,... | collective-permute-start | bytes 405512 | tf_op jit(solution)/shard_map/ppermute | solution.py:313
where the time goes:
time: 36.9 us; the launch traced here: 36.7 us
  starting transfers between devices  19.3 us (52%)
  waiting for transfers between devices  12.4 us (34%)
  Pallas kernels  4.86 us (13%)
    ppermute x15, starting transfers between devices, swap(): lax.ppermute(array, axis, [(place, place ^ step) for place in range(count)])  19.3 us
    ppermute x15, waiting for transfers between devices, swap(): lax.ppermute(array, axis, [(place, place ^ step) for place in range(count)])  12.4 us
    pallas_call x1, Pallas kernels, on_device(): pl.pallas_call(state_kernel, out_shape=messages * parts, in_specs=[hbm] *...  1.44 us
    pallas_call x1, Pallas kernels, on_device(): pl.pallas_call(last_kernel, out_shape=output, out_specs=hbm, scratch_shap...  1.08 us
    pallas_call x2, Pallas kernels, on_device(): pl.pallas_call(functools.partial(part_kernel, steps), out_shape=(column,)...  1.01 us
    pallas_call x1, Pallas kernels, on_device(): pl.pallas_call(inner_kernel, out_shape=(jax.ShapeDtypeStruct((heads, leng...  0.87 us
  transfers between devices with their start and end apart: 15, of which 8 were waited for; matrix products, arithmetic and copies ran while one was open for 0% of the time, Pallas kernels for 6%

commit v1 on v0

--- a/solution.py
+++ b/solution.py
@@ -357,7 +357,7 @@
     pieces = [exchange(own[part * heads : (part + 1) * heads]) for part in range(parts)]
     totals = []
     for part, chunk in enumerate(pieces):
-        order = list(range(heads)) if part else [0, heads - 1, *range(1, heads - 1)]
+        order = list(range(heads)) if part else [0, *range(heads - 1, 0, -1)]
         totals.append(
             pl.pallas_call(
                 functools.partial(quad_kernel, order),

time: 36.9 us -> 37 us (level)
  transfers between devices with their start and end apart: 15 -> 15, of which waited for: 8 -> 7; matrix products, arithmetic and copies ran while one was open for 0% -> 0% of each run, Pallas kernels for 6% -> 6%
where the time goes in v1:
time: 37 us; the launch traced here: 36.8 us
  starting transfers between devices  19.2 us (52%)
  waiting for transfers between devices  12.6 us (34%)
  Pallas kernels  4.87 us (13%)
    ppermute x15, starting transfers between devices, swap(): lax.ppermute(array, axis, [(place, place ^ step) for place in range(count)])  19.2 us
    ppermute x15, waiting for transfers between devices, swap(): lax.ppermute(array, axis, [(place, place ^ step) for place in range(count)])  12.6 us
    pallas_call x1, Pallas kernels, on_device(): pl.pallas_call(state_kernel, out_shape=messages * parts, in_specs=[hbm] *...  1.44 us
    pallas_call x1, Pallas kernels, on_device(): pl.pallas_call(last_kernel, out_shape=output, out_specs=hbm, scratch_shap...  1.08 us
    pallas_call x2, Pallas kernels, on_device(): pl.pallas_call(functools.partial(part_kernel, steps), out_shape=(column,)...  1.01 us
    pallas_call x1, Pallas kernels, on_device(): pl.pallas_call(inner_kernel, out_shape=(jax.ShapeDtypeStruct((heads, leng...  0.87 us
  transfers between devices with their start and end apart: 15, of which 7 were waited for; matrix products, arithmetic and copies ran while one was open for 0% of the time, Pallas kernels for 6%

profile of v1, /device:TPU:0, one launch (start us, length us, event | category | flops | bytes accessed | tf_op | source)
XLA Modules:
  0.0 36.8 jit_solution(6087657560306465451)
XLA Ops:
  0.0 1.4 %shard_map.56 = (f32[136,128]{1,0:T(8,128)S(1)}, f32[136,128]{1,0:T(8,128)S(1)}, f32[136,128]{1,0:T(8,128)S(1)}, f32[136,128]{1,0:T(8,128)S(1)}, f32[136,128]{1,...) custom-call(bf16[128,512]{1,0:T(8,128)(2,1)} %k_hbm.1, ...), custom_call_target="tpu_custom_call" | custom-call | tf_op jit(solution)/shard_map/pallas_call | solution.py:341
  1.5 3.0 %collective-permute-start.6 = (f32[136,128]{1,0:T(8,128)S(1)}, f32[136,128]{1,0:T(8,128)S(1)}, u32[]{:S(2)}, u32[]{:S(2)}) collective-permute-start(f32[136,128]{1,0:T(8,128)S(1)} %get-tuple-element.39), channel_id=1, source_target_pairs={{0,1},{1,0},{2,3},{3,2},{4,5},{5,4},{6,7},{7,6},{8,9},{9,8},{10,11... | collective-permute-start | bytes 208904 | tf_op jit(solution)/shard_map/ppermute | solution.py:313
  4.5 1.6 %collective-permute-start.7 = (f32[136,128]{1,0:T(8,128)S(1)}, f32[136,128]{1,0:T(8,128)S(1)}, u32[]{:S(2)}, u32[]{:S(2)}) collective-permute-start(f32[136,128]{1,0:T(8,128)S(1)} %get-tuple-element.40), channel_id=1, source_target_pairs={{0,2},{1,3},{2,0},{3,1},{4,6},{5,7},{6,4},{7,5},{8,10},{9,11},{10,... | collective-permute-start | bytes 208904 | tf_op jit(solution)/shard_map/ppermute | solution.py:313
  6.1 0.0 collective-permute-start.8
  6.1 2.9 %collective-permute-start = (f32[136,128]{1,0:T(8,128)S(1)}, f32[136,128]{1,0:T(8,128)S(1)}, u32[]{:S(2)}, u32[]{:S(2)}) collective-permute-start(f32[136,128]{1,0:T(8,128)S(1)} %get-tuple-element.32), channel_id=1, source_target_pairs={{0,3},{1,2},{2,1},{3,0},{4,7},{5,6},{6,5},{7,4},{8,11},{9,10},{10,... | collective-permute-start | bytes 208904 | tf_op jit(solution)/shard_map/ppermute | solution.py:313
  9.0 0.4 %collective-permute-start.1 = (f32[136,128]{1,0:T(8,128)S(1)}, f32[136,128]{1,0:T(8,128)S(1)}, u32[]{:S(2)}, u32[]{:S(2)}) collective-permute-start(f32[136,128]{1,0:T(8,128)S(1)} %get-tuple-element.33), channel_id=1, source_target_pairs={{0,2},{1,3},{2,0},{3,1},{4,6},{5,7},{6,4},{7,5},{8,10},{9,11},{10,... | collective-permute-start | bytes 208904 | tf_op jit(solution)/shard_map/ppermute | solution.py:313
  9.4 0.0 collective-permute-done.6.refs_1_.refs_9_
  9.4 0.1 collective-permute-start.2
  9.6 0.0 collective-permute-done.7.refs_2_.refs_10_
  9.6 2.3 %collective-permute-done.8.refs_3_.refs_11_ = f32[136,128]{1,0:T(8,128)S(1)} collective-permute-done((f32[136,128]{1,0:T(8,128)S(1)}, f32[136,128]{1,0:T(8,128)S(1)}, u32[]{:S(2)}, u32[]{:S(2)}) %collective-permute-start.8) | collective-permute-done | bytes 69664 | tf_op jit(solution)/shard_map/ppermute | solution.py:313
  11.9 0.1 shard_map.60.refs_0_
  12.0 2.7 %collective-permute-start.9 = (f32[136,128]{1,0:T(8,128)S(1)}, f32[136,128]{1,0:T(8,128)S(1)}, u32[]{:S(2)}, u32[]{:S(2)}) collective-permute-start(f32[136,128]{1,0:T(8,128)S(1)} %shard_map.60.refs_0_), channel_id=1, source_target_pairs={{0,4},{1,5},{2,6},{3,7},{4,0},{5,1},{6,2},{7,3},{8,12},{9,13},{10,... | collective-permute-start | bytes 208904 | tf_op jit(solution)/shard_map/ppermute | solution.py:313
  14.7 0.0 collective-permute-done.refs_1_.refs_7_
  14.7 0.0 collective-permute-done.1.refs_2_.refs_6_
  14.7 0.0 collective-permute-done.2.refs_3_.refs_5_
  14.7 0.1 shard_map.57.refs_0_
  14.7 1.9 %collective-permute-start.3 = (f32[136,128]{1,0:T(8,128)S(1)}, f32[136,128]{1,0:T(8,128)S(1)}, u32[]{:S(2)}, u32[]{:S(2)}) collective-permute-start(f32[136,128]{1,0:T(8,128)S(1)} %shard_map.57.refs_0_), channel_id=1, source_target_pairs={{0,4},{1,5},{2,6},{3,7},{4,0},{5,1},{6,2},{7,3},{8,12},{9,13},{10,... | collective-permute-start | bytes 208904 | tf_op jit(solution)/shard_map/ppermute | solution.py:313
  16.7 2.8 %collective-permute-done.9.refs_1_ = f32[136,128]{1,0:T(8,128)S(1)} collective-permute-done((f32[136,128]{1,0:T(8,128)S(1)}, f32[136,128]{1,0:T(8,128)S(1)}, u32[]{:S(2)}, u32[]{:S(2)}) %collective-permute-start.9) | collective-permute-done | bytes 69664 | tf_op jit(solution)/shard_map/ppermute | solution.py:313
  19.5 0.1 collective-permute-start.10
  19.6 1.4 %collective-permute-done.3.refs_1_ = f32[136,128]{1,0:T(8,128)S(1)} collective-permute-done((f32[136,128]{1,0:T(8,128)S(1)}, f32[136,128]{1,0:T(8,128)S(1)}, u32[]{:S(2)}, u32[]{:S(2)}) %collective-permute-start.3) | collective-permute-done | bytes 69664 | tf_op jit(solution)/shard_map/ppermute | solution.py:313
  21.0 0.1 collective-permute-start.4
  21.1 0.0 collective-permute-done.10.refs_1_
  21.1 1.6 %collective-permute-start.11 = (f32[136,128]{1,0:T(8,128)S(1)}, f32[136,128]{1,0:T(8,128)S(1)}, u32[]{:S(2)}, u32[]{:S(2)}) collective-permute-start(f32[136,128]{1,0:T(8,128)S(1)} %get-tuple-element.44), channel_id=1, source_target_pairs={{0,16},{8,24},{16,0},{24,8},{1,17},{9,25},{17,1},{25,9},{2,18},{10... | collective-permute-start | bytes 208904 | tf_op jit(solution)/shard_map/ppermute | solution.py:313
  22.7 0.0 collective-permute-done.4.refs_1_
  22.7 1.2 %collective-permute-start.5 = (f32[136,128]{1,0:T(8,128)S(1)}, f32[136,128]{1,0:T(8,128)S(1)}, u32[]{:S(2)}, u32[]{:S(2)}) collective-permute-start(f32[136,128]{1,0:T(8,128)S(1)} %get-tuple-element.37), channel_id=1, source_target_pairs={{0,16},{8,24},{16,0},{24,8},{1,17},{9,25},{17,1},{25,9},{2,18},{10... | collective-permute-start | bytes 208904 | tf_op jit(solution)/shard_map/ppermute | solution.py:313
  23.9 2.0 %collective-permute-done.11.refs_1_ = f32[136,128]{1,0:T(8,128)S(1)} collective-permute-done((f32[136,128]{1,0:T(8,128)S(1)}, f32[136,128]{1,0:T(8,128)S(1)}, u32[]{:S(2)}, u32[]{:S(2)}) %collective-permute-start.11) | collective-permute-done | bytes 69664 | tf_op jit(solution)/shard_map/ppermute | solution.py:313
  25.9 1.3 %collective-permute-done.5.refs_0_ = f32[136,128]{1,0:T(8,128)S(1)} collective-permute-done((f32[136,128]{1,0:T(8,128)S(1)}, f32[136,128]{1,0:T(8,128)S(1)}, u32[]{:S(2)}, u32[]{:S(2)}) %collective-permute-start.5) | collective-permute-done | bytes 69664 | tf_op jit(solution)/shard_map/ppermute | solution.py:313
  27.2 0.0 copy-start
  27.2 0.0 copy-start.1
  27.2 0.0 copy-start.2
  27.2 0.2 shard_map.63
  27.5 0.0 copy-start.4
  27.5 0.0 copy-start.3
  27.5 0.1 collective-permute-start.14
  27.6 0.8 %collective-permute-start.13 = (f32[264,128]{1,0:T(8,128)S(1)}, f32[264,128]{1,0:T(8,128)S(1)}, u32[]{:S(2)}, u32[]{:S(2)}) collective-permute-start(f32[264,128]{1,0:T(8,128)S(1)} %get-tuple-element.49), channel_id=1, source_target_pairs={{0,1},{1,0},{2,3},{3,2},{4,5},{5,4},{6,7},{7,6},{8,9},{9,8},{10,11... | collective-permute-start | bytes 405512 | tf_op jit(solution)/shard_map/ppermute | solution.py:313
  28.4 2.7 %collective-permute-start.12 = (f32[264,128]{1,0:T(8,128)S(1)}, f32[264,128]{1,0:T(8,128)S(1)}, u32[]{:S(2)}, u32[]{:S(2)}) collective-permute-start(f32[264,128]{1,0:T(8,128)S(1)} %get-tuple-element.47), channel_id=1, source_target_pairs={{0,3},{1,2},{2,1},{3,0},{4,7},{5,6},{6,5},{7,4},{8,11},{9,10},{10,... | collective-permute-start | bytes 405512 | tf_op jit(solution)/shard_map/ppermute | solution.py:313
  31.1 0.0 copy-done
  31.1 0.0 copy-done.1
  31.1 0.0 copy-done.2
  31.1 0.0 copy-done.4
  31.1 0.0 copy-done.3
  31.1 0.9 %shard_map.55 = (f32[4,128,256]{2,1,0:T(8,128)S(1)}, f32[4,128,3]{2,1,0:T(8,128)S(1)}) custom-call(bf16[128,512]{1,0:T(8,128)(2,1)S(1)} %copy-done, bf16[128,512]{1,0:T(8,128)(2,1)S(1)} %copy-done.2, bf16[128,1024]{1,0:T(8,128)(2,1)S(1)} %copy-done.1, f32[4,128]{1,0:T(4,128)S(1)} %copy-done.3, f32[4,128]{1,0:T(4,128)S(1)} %copy-done.4), custom_call_target="tpu_custom_call" | custom-call | tf_op jit(solution)/shard_map/pallas_call | solution.py:349
  32.0 2.1 %collective-permute-done.14.refs_0_ = f32[264,128]{1,0:T(8,128)S(1)} collective-permute-done((f32[264,128]{1,0:T(8,128)S(1)}, f32[264,128]{1,0:T(8,128)S(1)}, u32[]{:S(2)}, u32[]{:S(2)}) %collective-permute-start.14) | collective-permute-done | bytes 135200 | tf_op jit(solution)/shard_map/ppermute | solution.py:313
  34.1 0.4 %shard_map.65.refs_2_ = bf16[128,256]{1,0:T(8,128)(2,1)S(1)} custom-call(bf16[128,512]{1,0:T(8,128)(2,1)S(1)} %copy-done, f32[4,128,256]{2,1,0:T(8,128)S(1)} %get-tuple-element.29.num_ref, f32[4,128,3]{2,1,0:T(8,128)S(1)} %get-tuple-element.30.stat_ref, f32[264,128]{1,0:T(8,128)S(1)} %collective-permute-done.14.refs_0_), custom_call_target="tpu_custom_call" | custom-call | tf_op jit(solution)/shard_map/pallas_call | solution.py:393
  34.5 0.0 collective-permute-done.13.refs_1_
  34.5 0.6 %shard_map.64 = (bf16[128,256]{1,0:T(8,128)(2,1)S(1)}, bf16[128,256]{1,0:T(8,128)(2,1)S(1)}) custom-call(bf16[128,512]{1,0:T(8,128)(2,1)S(1)} %copy-done, f32[4,128,256]{2,1,0:T(8,128)S(1)} %get-tuple-element.29.num_ref, f32[4,128,3]{2,1,0:T(8,128)S(1)} %get-tuple-element.30.stat_ref, f32[264,128]{1,0:T(8,128)S(1)} %get-tuple-element.48.refs_0_, ...), custom_call_target="tpu_custom_call" | custom-call | tf_op jit(solution)/shard_map/pallas_call | solution.py:393
  35.1 0.6 %collective-permute-done.12.message_ref = f32[264,128]{1,0:T(8,128)S(1)} collective-permute-done((f32[264,128]{1,0:T(8,128)S(1)}, f32[264,128]{1,0:T(8,128)S(1)}, u32[]{:S(2)}, u32[]{:S(2)}) %collective-permute-start.12) | collective-permute-done | bytes 135200 | tf_op jit(solution)/shard_map/ppermute | solution.py:313
  35.7 1.1 %shard_map.66 = bf16[128,1024]{1,0:T(8,128)(2,1)} custom-call(bf16[128,512]{1,0:T(8,128)(2,1)S(1)} %copy-done, f32[4,128,256]{2,1,0:T(8,128)S(1)} %get-tuple-element.29.num_ref, f32[4,128,3]{2,1,0:T(8,128)S(1)} %get-tuple-element.30.stat_ref, f32[264,128]{1,0:T(8,128)S(1)} %collective-permute-done.12.message_ref, ...), custom_call_target="tpu_custom_call" | custom-call | tf_op jit(solution)/shard_map/pallas_call | solution.py:398
  (4 shorter events, 0.1 us)
Async XLA Ops:
  1.5 8.0 %collective-permute-start.6 = (f32[136,128]{1,0:T(8,128)S(1)}, f32[136,128]{1,0:T(8,128)S(1)}, u32[]{:S(2)}, u32[]{:S(2)}) collective-permute-start(f32[136,128]{1,0:T(8,128)S(1)} %get-tuple-element.39), channel_id=1, source_target_pairs={{0,1},{1,0},{2,3},{3,2},{4,5},{5,4},{6,7},{7,6},{8,9},{9,8},{10,11... | collective-permute-start | bytes 208904 | tf_op jit(solution)/shard_map/ppermute | solution.py:313
  4.5 5.1 %collective-permute-start.7 = (f32[136,128]{1,0:T(8,128)S(1)}, f32[136,128]{1,0:T(8,128)S(1)}, u32[]{:S(2)}, u32[]{:S(2)}) collective-permute-start(f32[136,128]{1,0:T(8,128)S(1)} %get-tuple-element.40), channel_id=1, source_target_pairs={{0,2},{1,3},{2,0},{3,1},{4,6},{5,7},{6,4},{7,5},{8,10},{9,11},{10,... | collective-permute-start | bytes 208904 | tf_op jit(solution)/shard_map/ppermute | solution.py:313
  6.1 5.9 %collective-permute-start.8 = (f32[136,128]{1,0:T(8,128)S(1)}, f32[136,128]{1,0:T(8,128)S(1)}, u32[]{:S(2)}, u32[]{:S(2)}) collective-permute-start(f32[136,128]{1,0:T(8,128)S(1)} %get-tuple-element.41), channel_id=1, source_target_pairs={{0,3},{1,2},{2,1},{3,0},{4,7},{5,6},{6,5},{7,4},{8,11},{9,10},{10,... | collective-permute-start | bytes 208904 | tf_op jit(solution)/shard_map/ppermute | solution.py:313
  6.1 8.6 %collective-permute-start = (f32[136,128]{1,0:T(8,128)S(1)}, f32[136,128]{1,0:T(8,128)S(1)}, u32[]{:S(2)}, u32[]{:S(2)}) collective-permute-start(f32[136,128]{1,0:T(8,128)S(1)} %get-tuple-element.32), channel_id=1, source_target_pairs={{0,3},{1,2},{2,1},{3,0},{4,7},{5,6},{6,5},{7,4},{8,11},{9,10},{10,... | collective-permute-start | bytes 208904 | tf_op jit(solution)/shard_map/ppermute | solution.py:313
  9.0 5.7 %collective-permute-start.1 = (f32[136,128]{1,0:T(8,128)S(1)}, f32[136,128]{1,0:T(8,128)S(1)}, u32[]{:S(2)}, u32[]{:S(2)}) collective-permute-start(f32[136,128]{1,0:T(8,128)S(1)} %get-tuple-element.33), channel_id=1, source_target_pairs={{0,2},{1,3},{2,0},{3,1},{4,6},{5,7},{6,4},{7,5},{8,10},{9,11},{10,... | collective-permute-start | bytes 208904 | tf_op jit(solution)/shard_map/ppermute | solution.py:313
  9.4 5.2 %collective-permute-start.2 = (f32[136,128]{1,0:T(8,128)S(1)}, f32[136,128]{1,0:T(8,128)S(1)}, u32[]{:S(2)}, u32[]{:S(2)}) collective-permute-start(f32[136,128]{1,0:T(8,128)S(1)} %get-tuple-element.34), channel_id=1, source_target_pairs={{0,1},{1,0},{2,3},{3,2},{4,5},{5,4},{6,7},{7,6},{8,9},{9,8},{10,11... | collective-permute-start | bytes 208904 | tf_op jit(solution)/shard_map/ppermute | solution.py:313
  12.0 7.5 %collective-permute-start.9 = (f32[136,128]{1,0:T(8,128)S(1)}, f32[136,128]{1,0:T(8,128)S(1)}, u32[]{:S(2)}, u32[]{:S(2)}) collective-permute-start(f32[136,128]{1,0:T(8,128)S(1)} %shard_map.60.refs_0_), channel_id=1, source_target_pairs={{0,4},{1,5},{2,6},{3,7},{4,0},{5,1},{6,2},{7,3},{8,12},{9,13},{10,... | collective-permute-start | bytes 208904 | tf_op jit(solution)/shard_map/ppermute | solution.py:313
  14.7 6.2 %collective-permute-start.3 = (f32[136,128]{1,0:T(8,128)S(1)}, f32[136,128]{1,0:T(8,128)S(1)}, u32[]{:S(2)}, u32[]{:S(2)}) collective-permute-start(f32[136,128]{1,0:T(8,128)S(1)} %shard_map.57.refs_0_), channel_id=1, source_target_pairs={{0,4},{1,5},{2,6},{3,7},{4,0},{5,1},{6,2},{7,3},{8,12},{9,13},{10,... | collective-permute-start | bytes 208904 | tf_op jit(solution)/shard_map/ppermute | solution.py:313
  19.5 1.6 %collective-permute-start.10 = (f32[136,128]{1,0:T(8,128)S(1)}, f32[136,128]{1,0:T(8,128)S(1)}, u32[]{:S(2)}, u32[]{:S(2)}) collective-permute-start(f32[136,128]{1,0:T(8,128)S(1)} %get-tuple-element.42.refs_0_), channel_id=1, source_target_pairs={{0,8},{8,0},{16,24},{24,16},{1,9},{9,1},{17,25},{25,17},{2,10},{10... | collective-permute-start | bytes 208904 | tf_op jit(solution)/shard_map/ppermute | solution.py:313
  21.0 1.7 %collective-permute-start.4 = (f32[136,128]{1,0:T(8,128)S(1)}, f32[136,128]{1,0:T(8,128)S(1)}, u32[]{:S(2)}, u32[]{:S(2)}) collective-permute-start(f32[136,128]{1,0:T(8,128)S(1)} %get-tuple-element.35.refs_0_), channel_id=1, source_target_pairs={{0,8},{8,0},{16,24},{24,16},{1,9},{9,1},{17,25},{25,17},{2,10},{10... | collective-permute-start | bytes 208904 | tf_op jit(solution)/shard_map/ppermute | solution.py:313
  21.1 4.8 %collective-permute-start.11 = (f32[136,128]{1,0:T(8,128)S(1)}, f32[136,128]{1,0:T(8,128)S(1)}, u32[]{:S(2)}, u32[]{:S(2)}) collective-permute-start(f32[136,128]{1,0:T(8,128)S(1)} %get-tuple-element.44), channel_id=1, source_target_pairs={{0,16},{8,24},{16,0},{24,8},{1,17},{9,25},{17,1},{25,9},{2,18},{10... | collective-permute-start | bytes 208904 | tf_op jit(solution)/shard_map/ppermute | solution.py:313
  22.7 4.5 %collective-permute-start.5 = (f32[136,128]{1,0:T(8,128)S(1)}, f32[136,128]{1,0:T(8,128)S(1)}, u32[]{:S(2)}, u32[]{:S(2)}) collective-permute-start(f32[136,128]{1,0:T(8,128)S(1)} %get-tuple-element.37), channel_id=1, source_target_pairs={{0,16},{8,24},{16,0},{24,8},{1,17},{9,25},{17,1},{25,9},{2,18},{10... | collective-permute-start | bytes 208904 | tf_op jit(solution)/shard_map/ppermute | solution.py:313
  27.2 3.8 %copy-start = (bf16[128,512]{1,0:T(8,128)(2,1)S(1)}, bf16[128,512]{1,0:T(8,128)(2,1)}, u32[]{:S(2)}) copy-start(bf16[128,512]{1,0:T(8,128)(2,1)} %q_ref.7) | copy-start | bytes 393220
  27.2 3.8 %copy-start.1 = (bf16[128,1024]{1,0:T(8,128)(2,1)S(1)}, bf16[128,1024]{1,0:T(8,128)(2,1)}, u32[]{:S(2)}) copy-start(bf16[128,1024]{1,0:T(8,128)(2,1)} %v_hbm.1) | copy-start | bytes 786436
  27.2 3.8 %copy-start.2 = (bf16[128,512]{1,0:T(8,128)(2,1)S(1)}, bf16[128,512]{1,0:T(8,128)(2,1)}, u32[]{:S(2)}) copy-start(bf16[128,512]{1,0:T(8,128)(2,1)} %k_hbm.1) | copy-start | bytes 393220
  27.5 3.6 %copy-start.4 = (f32[4,128]{1,0:T(4,128)S(1)}, f32[4,128]{1,0:T(4,128)}, u32[]{:S(2)}) copy-start(f32[4,128]{1,0:T(4,128)} %fo_hbm.1) | copy-start | bytes 6148
  27.5 3.6 %copy-start.3 = (f32[4,128]{1,0:T(4,128)S(1)}, f32[4,128]{1,0:T(4,128)}, u32[]{:S(2)}) copy-start(f32[4,128]{1,0:T(4,128)} %in_hbm.1) | copy-start | bytes 6148
  27.5 6.6 %collective-permute-start.14 = (f32[264,128]{1,0:T(8,128)S(1)}, f32[264,128]{1,0:T(8,128)S(1)}, u32[]{:S(2)}, u32[]{:S(2)}) collective-permute-start(f32[264,128]{1,0:T(8,128)S(1)} %get-tuple-element.52), channel_id=1, source_target_pairs={{0,2},{1,3},{2,0},{3,1},{4,6},{5,7},{6,4},{7,5},{8,10},{9,11},{10,... | collective-permute-start | bytes 405512 | tf_op jit(solution)/shard_map/ppermute | solution.py:313
  27.6 6.9 %collective-permute-start.13 = (f32[264,128]{1,0:T(8,128)S(1)}, f32[264,128]{1,0:T(8,128)S(1)}, u32[]{:S(2)}, u32[]{:S(2)}) collective-permute-start(f32[264,128]{1,0:T(8,128)S(1)} %get-tuple-element.49), channel_id=1, source_target_pairs={{0,1},{1,0},{2,3},{3,2},{4,5},{5,4},{6,7},{7,6},{8,9},{9,8},{10,11... | collective-permute-start | bytes 405512 | tf_op jit(solution)/shard_map/ppermute | solution.py:313
  28.4 7.3 %collective-permute-start.12 = (f32[264,128]{1,0:T(8,128)S(1)}, f32[264,128]{1,0:T(8,128)S(1)}, u32[]{:S(2)}, u32[]{:S(2)}) collective-permute-start(f32[264,128]{1,0:T(8,128)S(1)} %get-tuple-element.47), channel_id=1, source_target_pairs={{0,3},{1,2},{2,1},{3,0},{4,7},{5,6},{6,5},{7,4},{8,11},{9,10},{10,... | collective-permute-start | bytes 405512 | tf_op jit(solution)/shard_map/ppermute | solution.py:313
